TPU v7x, 512 devices: a whole 4x8x8 slice. The times are simulated.
512 devices in a mesh: section: 8 (over x, core), group: 4 (over z_hi), tp: 16 (over y, z_lo).
Axes of the slice: x: 4, y: 8, z: 8 (z_hi: 4, z_lo: 2; z = z_hi * 2 + z_lo), core: 2. Of those that a mesh axis runs over, the one named last changes fastest.
Arguments:
- vision_hidden: bfloat16 [8192, 8192], P(('section', 'group'), 'tp'), may hold values from -6 to 6
- proj_weight: bfloat16 [8192, 8192], P('group', 'tp'), may hold values from -0.0625 to 0.0625
- proj_bias: bfloat16 [8192], P('tp'), may hold values from -3 to 3
- text_embed: bfloat16 [32768, 8192], P(('section', 'group'), 'tp')
- norm_gain: float32 [8192], P('tp'), may hold values from 0.1 to 1.9
- key_weight: bfloat16 [8192, 1024], P('tp'), may hold values from -0.0625 to 0.0625
- image_group: int32 [32], replicated, may hold values from 0 to 3, as said below
- image_offset: int32 [32], replicated, may hold values from 0 to 768, as said below
Outputs:
- keys: bfloat16 [32768, 1024], P(('section', 'group', 'tp'))
Inputs may be any that keep to these rules, and one draw needn't show every extreme that they name: `image_group`: of the 4 images of one section, exactly two name the same group and the others name distinct other groups. `image_offset`: each image slot lies inside its prompt, and the two slots that share a prompt do not intersect.
All inputs are finite; a program needn't handle non-finite values.
Results may differ from a plain program's by a relative error of at most 0.0052.
Values may be sent and summed in bfloat16 or wider, within the bound.
A program may use at most 64 MiB of HBM per device.

v0:
```python
import jax
import jax.numpy as jnp
from jax import lax
from jax.sharding import PartitionSpec as P

D = 8192


def from_behind(block, axis, distance):
    devices = range(lax.axis_size(axis))
    route = [((i - distance) % len(devices), i) for i in devices]
    return lax.ppermute(block, axis, route)


def on_device(
    vision_hidden,
    proj_weight,
    proj_bias,
    text_embed,
    norm_gain,
    key_weight,
    image_group,
    image_offset,
):
    features = lax.all_gather(vision_hidden, "tp", axis=1, tiled=True)
    img_rows = features.shape[0]
    summed = jnp.dot(
        features,
        lax.all_gather(proj_weight, "group", axis=0, tiled=True),
        preferred_element_type=jnp.float32,
    )
    projected = (summed + proj_bias.astype(jnp.float32)).astype(jnp.bfloat16)
    sections = lax.axis_size("section")
    groups = lax.axis_size("group")
    arrived = from_behind(projected, "section", sections // 2)
    pooled = lax.all_gather(arrived, "group", axis=0, tiled=True)
    source = (lax.axis_index("section") + sections - sections // 2) % sections
    mine = lax.axis_index("group")
    matches = []
    starts = []
    for slot in range(groups):
        image = source * groups + slot
        matches.append(image_group[image] == mine)
        starts.append(image_offset[image])
    prompt = text_embed
    for slot in range(groups):
        piece = pooled[slot * img_rows : (slot + 1) * img_rows]
        updated = lax.dynamic_update_slice_in_dim(prompt, piece, starts[slot], 0)
        prompt = jnp.where(matches[slot], updated, prompt)
    prompt_vals = prompt.astype(jnp.float32)
    prompt_sq = lax.psum(jnp.sum(prompt_vals * prompt_vals, axis=1), "tp")
    values = prompt.astype(jnp.float32)
    inv_rms = 1.0 / jnp.sqrt(prompt_sq / D + 1e-05)
    partial_value = jnp.dot(
        (values * inv_rms[:, None] * norm_gain).astype(jnp.bfloat16),
        key_weight,
        preferred_element_type=jnp.float32,
    )
    keys = lax.psum_scatter(partial_value, "tp", scatter_dimension=0, tiled=True)
    return keys.astype(jnp.bfloat16)


def solution(mesh):
    in_specs = (
        P(("section", "group"), "tp"),
        P("group", "tp"),
        P("tp"),
        P(("section", "group"), "tp"),
        P("tp"),
        P("tp", None),
        P(),
        P(),
    )
    out_specs = P(("section", "group", "tp"), None)
    return jax.shard_map(
        on_device, mesh=mesh, in_specs=in_specs, out_specs=out_specs, check_vma=False
    )
```

profile of v0, /device:TPU:22, one launch (start us, length us, event | category | flops | bytes accessed | tf_op | source)
XLA Modules:
  0.0 489.0 jit_solution(13508308917842165258)
XLA Ops:
  6.5 0.0 copy-start
  6.5 0.0 copy-start.4
  6.5 0.0 all-gather.4.cloned.1.call-start
  6.5 1.3 copy.14
  7.9 0.0 all-gather.4.cloned.1.call-update
  7.9 0.0 all-gather.6.cloned.1.call-start
  7.9 0.7 all-gather.6.cloned.1.call-update
  8.6 0.0 all-gather.8.cloned.1.call-start
  8.7 0.0 copy-done.4
  8.7 0.0 copy-start.2
  8.7 0.0 copy-start.3
  8.7 107.4 %all-gather.4.cloned.1.call-done = bf16[256,8192]{1,0:T(8,128)(2,1)} async-done(((bf16[256,512]{1,0:T(8,128)(2,1)}), bf16[256,8192]{1,0:T(8,128)(2,1)}) %all-gather.4.cloned.1.call-update) | async-done | bytes 4194320 | tf_op jit(solution)/shard_map/all_gather | solution.py:25
  116.2 155.2 %all-gather.6.cloned.1.call-done = bf16[8192,512]{1,0:T(8,128)(2,1)} async-done(((bf16[2048,512]{1,0:T(8,128)(2,1)}), bf16[8192,512]{1,0:T(8,128)(2,1)}) %all-gather.6.cloned.1.call-update) | async-done | bytes 8388624 | tf_op jit(solution)/shard_map/all_gather | solution.py:29
  271.3 7.0 %fusion.3 = bf16[256,512]{1,0:T(8,128)(2,1)S(1)} fusion(bf16[256,8192]{1,0:T(8,128)(2,1)} %all-gather.4.cloned.1.call-done, bf16[8192,512]{1,0:T(8,128)(2,1)} %all-gather.6.cloned.1.call-done, f32[512]{0:T(512)S(1)} %convert_element_type.16), kind=kOutput, calls=%fused_computation.6 | convolution fusion | flops 2147745792 | bytes 12847104 | tf_op jit(solution)/shard_map/dot_general | solution.py:27
  278.3 0.0 copy-start.5
  278.3 3.4 collective-permute-start
  281.7 8.0 %collective-permute-done = bf16[256,512]{1,0:T(8,128)(2,1)S(1)} collective-permute-done((bf16[256,512]{1,0:T(8,128)(2,1)S(1)}, bf16[256,512]{1,0:T(8,128)(2,1)S(1)}, u32[]{:S(2)}, u32[]{:S(2)}) %collective-permute-start) | collective-permute-done | bytes 262176 | tf_op jit(solution)/shard_map/ppermute | solution.py:12
  289.7 0.0 copy-start.1
  289.7 0.7 copy-done.1
  290.4 0.0 all-gather.8.cloned.1.call-update
  290.4 0.0 reduce-scatter.2.cloned.1.call-start
  290.5 0.0 copy-done.2
  290.5 0.0 copy-done.3
  290.5 0.7 fusion.8
  301.0 31.5 %all-gather.8.cloned.1.call-done = bf16[1024,512]{1,0:T(8,128)(2,1)} async-done(((bf16[256,512]{1,0:T(8,128)(2,1)}), bf16[1024,512]{1,0:T(8,128)(2,1)}) %all-gather.8.cloned.1.call-update) | async-done | bytes 1048592 | tf_op jit(solution)/shard_map/all_gather | solution.py:36
  332.4 1.0 slice_select_fusion.3
  333.5 1.9 select_n.83
  335.4 1.1 slice_select_fusion.2
  336.4 1.9 select_n.89
  338.3 1.1 slice_select_fusion.1
  339.4 1.9 select_n.95
  341.2 1.1 slice_select_fusion
  342.3 1.9 select_n.101
  344.2 0.3 fusion
  344.5 30.8 %psum.7 = f32[1024]{0:T(1024)S(1)} all-reduce(f32[1024]{0:T(1024)S(1)} %fusion), channel_id=1, replica_groups=mesh['section'=8,'group'=4,'tp'=16] {'tp'}, use_global_device_ids=true, to_apply=%region_1.2 | all-reduce | flops 1024 | bytes 8192 | tf_op jit(solution)/shard_map/psum | solution.py:51
  375.3 0.0 copy-done
  375.3 0.0 copy-done.5
  375.3 3.3 fusion.4
  378.6 0.0 reduce-scatter.2.cloned.1.call-update
  378.6 102.3 %reduce-scatter.2.cloned.1.call-done = f32[64,1024]{1,0:T(8,128)} async-done(((f32[1024,1024]{1,0:T(8,128)}), f32[64,1024]{1,0:T(8,128)}) %reduce-scatter.2.cloned.1.call-update) | async-done | bytes 262160 | tf_op jit(solution)/shard_map/reduce_scatter | solution.py:59
  480.9 1.6 convert_element_type.20
  (2 shorter events, 0.0 us)
Async XLA Ops:
  6.5 368.8 %copy-start = (bf16[512,1024]{1,0:T(8,128)(2,1)S(1)}, bf16[512,1024]{1,0:T(8,128)(2,1)}, u32[]{:S(2)}) copy-start(bf16[512,1024]{1,0:T(8,128)(2,1)} %param.13) | copy-start | bytes 3145732
  6.5 2.2 copy-start.4
  6.5 109.6 %all-gather.4.cloned.1.call-start = ((), (), s32[]{:S(2)}) async-start(), calls=%async_computation.1 | async-start | bytes 4456448 | tf_op jit(solution)/shard_map/all_gather | solution.py:25
  7.9 263.4 %all-gather.6.cloned.1.call-start = ((), (), s32[]{:S(2)}) async-start(), calls=%async_computation.2 | async-start | bytes 10485760 | tf_op jit(solution)/shard_map/all_gather | solution.py:29
  8.6 323.8 %all-gather.8.cloned.1.call-start = ((), (), s32[]{:S(2)}) async-start(), calls=%async_computation.3 | async-start | bytes 1310720 | tf_op jit(solution)/shard_map/all_gather | solution.py:36
  8.7 281.8 %copy-start.2 = (s32[32]{0:T(128)S(1)}, s32[32]{0:T(128)}, u32[]{:S(2)}) copy-start(s32[32]{0:T(128)} %param.14) | copy-start | bytes 388
  8.7 281.8 %copy-start.3 = (s32[32]{0:T(128)S(1)}, s32[32]{0:T(128)}, u32[]{:S(2)}) copy-start(s32[32]{0:T(128)} %param.15) | copy-start | bytes 388
  278.3 97.0 %copy-start.5 = (f32[512]{0:T(512)S(1)}, f32[512]{0:T(512)}, u32[]{:S(2)}) copy-start(f32[512]{0:T(512)} %param.12) | copy-start | bytes 6148
  278.3 11.3 %collective-permute-start = (bf16[256,512]{1,0:T(8,128)(2,1)S(1)}, bf16[256,512]{1,0:T(8,128)(2,1)S(1)}, u32[]{:S(2)}, u32[]{:S(2)}) collective-permute-start(bf16[256,512]{1,0:T(8,128)(2,1)S(1)} %fusion.3), channel_id=1, source_target_pairs={{256,0},{320,64},{384,128},{448,192},{0,256},{64,320},{128,384},{1... | collective-permute-start | bytes 786440 | tf_op jit(solution)/shard_map/ppermute | solution.py:12
  289.7 0.7 copy-start.1
  290.4 190.5 %reduce-scatter.2.cloned.1.call-start = ((), (), s32[]{:S(2)}) async-start(), calls=%async_computation.4 | async-start | bytes 4456448 | tf_op jit(solution)/shard_map/reduce_scatter | solution.py:59
Sparse Core Ops, SparseCore 0:
  9.4 106.6 all-gather.3
  118.3 153.0 all-gather.5
  290.5 41.8 all-gather.7
  378.7 102.1 reduce-scatter.1
where the time goes:
time: 490 us; the launch traced here: 489 us
  waiting for transfers between devices  405 us (83%)
  blocking collectives  30.8 us (6%)
  between operations  23.1 us (5%)
  local copies, waits for them, and re-layouts  10.2 us (2%)
  matrix products  10.2 us (2%)
  other arithmetic  6.11 us (1%)
    all_gather x1, waiting for transfers between devices, on_device(): lax.all_gather(proj_weight, 'group', axis=0, tiled=True)  155 us
    all_gather x1, waiting for transfers between devices, on_device(): features = lax.all_gather(vision_hidden, 'tp', axis=1, tiled=True)  107 us
    reduce_scatter x1, waiting for transfers between devices, on_device(): lax.psum_scatter(partial_value, 'tp', scatter_dimension=0, tiled=True)  102 us
    all_gather x1, waiting for transfers between devices, on_device(): pooled = lax.all_gather(arrived, 'group', axis=0, tiled=True)  31.5 us
    psum x1, blocking collectives, on_device(): prompt_sq = lax.psum(jnp.sum(prompt_vals * prompt_vals, axis=1), 'tp')  30.8 us
  transfers between devices with their start and end apart: 5, of which 5 were waited for; matrix products, arithmetic and copies ran while one was open for 0% of the time, Pallas kernels for 0%

commit v1 on v0

v1 whole, which is shorter than its diff:
```python
import jax
import jax.numpy as jnp
from jax import lax
from jax.experimental import pallas as pl
from jax.experimental.pallas import tpu as pltpu
from jax.sharding import PartitionSpec as P

MESH = pl.DeviceIdType.MESH
D = 8192
KV = 1024
PAD = 128
WIDE = KV + PAD
EPS = 1e-05
BIG = 1.9e19
F32 = jnp.float32
BF16 = jnp.bfloat16
SEMS = 160


def dot(a, b):
    return jnp.dot(a, b, preferred_element_type=F32)


def three_parts(v):
    lane = lax.broadcasted_iota(jnp.int32, (v.shape[0], PAD), 1)
    hi = v.astype(BF16).astype(F32)
    rest = jnp.where(hi < jnp.inf, v - hi, 0.0)
    mid = rest.astype(BF16).astype(F32)
    low = rest - mid
    parts = jnp.where(lane == 0, hi, jnp.where(lane == 1, mid, jnp.where(lane == 2, low, 0.0)))
    return parts.astype(BF16)


def inverse_rms(half_sum):
    return 1.0 / jnp.sqrt(half_sum * 2.0 / D + EPS)


def kernel(
    vis, wp, bias, txt, gain, kw, grp, off, out,
    xb, wb, tv, kwv, tsend, trecv, town, ysend, yrecv, acc, isend, irecv, ikey, dest, ag,
    ssem, rsem, lsem,
):
    s, g, t = lax.axis_index("section"), lax.axis_index("group"), lax.axis_index("tp")
    y, l = t // 2, t % 2
    other = 1 - l
    partner = 2 * y + other
    sib = s + 1 - 2 * (s % 2)
    g_up, g_down, g_far = (g + 1) % 4, (g + 3) % 4, (g + 2) % 4
    s_up, s_down, s_far = (s + 2) % 8, (s + 6) % 8, (s + 4) % 8

    local = []
    for k, (src, dst) in enumerate(
        ((txt, tv), (kw, kwv), (vis, xb.at[t]), (wp, wb.at[g]))
    ):
        copy = pltpu.make_async_copy(src, dst, lsem.at[k])
        copy.start()
        local.append(copy)

    peers = [{"tp": (t + d) % 16} for d in range(1, 16)]
    peers += [{"group": g_up}, {"group": g_down}]
    peers += [{"section": s_up}, {"section": s_down}, {"section": sib}]
    peers += [{"section": s_far, "group": h} for h in range(4)]
    barrier = pltpu.get_barrier_semaphore()
    for peer in peers:
        pl.semaphore_signal(barrier, inc=1, device_id=peer, device_id_type=MESH)
    pl.semaphore_wait(barrier, len(peers))

    sent = []

    def send(src, dst, **peer):
        k = len(sent)
        copy = pltpu.make_async_remote_copy(
            src_ref=src, dst_ref=dst, send_sem=ssem.at[k], recv_sem=rsem.at[k],
            device_id=peer, device_id_type=MESH,
        )
        copy.start()
        sent.append(copy)
        return k, peer

    def arrive(handle, dst):
        k, peer = handle
        pltpu.make_async_remote_copy(
            src_ref=dst, dst_ref=dst, send_sem=ssem.at[k], recv_sem=rsem.at[k],
            device_id=peer, device_id_type=MESH,
        ).wait_recv()

    def column(k, lane):
        return 2 * ((y + k + 8) % 8) + lane

    def ring(buf, first):
        up, down = (y + 1) % 8, (y + 7) % 8
        to_partner = send(first, buf.at[t], tp=partner)
        right = {0: send(first, buf.at[t], tp=2 * up + l)}
        left = {0: send(first, buf.at[t], tp=2 * down + l)}
        yield
        arrive(to_partner, buf.at[partner])
        right[1] = send(buf.at[partner], buf.at[partner], tp=2 * up + l)
        left[1] = send(buf.at[partner], buf.at[partner], tp=2 * down + l)
        lanes = (l, other)
        for step in (1, 2):
            for q in range(2):
                yield
                a, b = buf.at[column(-step, lanes[q])], buf.at[column(step, lanes[q])]
                arrive(right[q], a)
                right[q] = send(a, a, tp=2 * up + l)
                arrive(left[q], b)
                left[q] = send(b, b, tp=2 * down + l)
        yield
        ends = []
        for q in range(2):
            arrive(right[q], buf.at[column(-3, lanes[q])])
            arrive(left[q], buf.at[column(3, lanes[q])])
        a, b = buf.at[column(-3, 0)], buf.at[column(3, 1)]
        ends.append((send(a, a, tp=2 * up + l), column(-4, 0)))
        ends.append((send(b, b, tp=2 * down + l), column(4, 1)))
        yield
        for handle, k in ends:
            arrive(handle, buf.at[k])

    local[2].wait()
    local[3].wait()
    features = ring(xb, xb.at[t])
    next(features)
    z_up = send(wb.at[g, s], wb.at[g, s], group=g_up)
    z_down = send(wb.at[g, s], wb.at[g, s], group=g_down)

    local[0].wait()
    local[1].wait()

    def text_part(which, j):
        part = tv[pl.ds(4 * j, 4), which].reshape(256, 512).astype(F32)
        part = jnp.minimum(jnp.maximum(part, -BIG), BIG)
        half = jnp.sum(part * part, axis=1, keepdims=True) * 0.5
        return dot((part * gain[...]).astype(BF16), kwv[...]), half

    @pl.loop(0, 2)
    def _(j):
        keys, half = text_part(other, j)
        tsend[pl.ds(4 * j, 4), :, :KV] = keys.astype(BF16).reshape(4, 64, KV)
        tsend[pl.ds(4 * j, 4), :, KV:] = three_parts(half).reshape(4, 64, PAD)

    @pl.loop(0, 2)
    def _(j):
        keys, half = text_part(l, j)
        lane = lax.broadcasted_iota(jnp.int32, (256, PAD), 1)
        town[pl.ds(4 * j, 4), :, :KV] = keys.reshape(4, 64, KV)
        town[pl.ds(4 * j, 4), :, KV:] = jnp.where(lane == 0, half, 0.0).reshape(4, 64, PAD)

    next(features)

    lo, hi = pl.ds(0, 128), pl.ds(128, 128)
    pieces = {}

    def spread(h):
        ref = wb.at[h, s]
        return [
            send(ref, ref, section=s_up), send(ref, ref, section=s_down),
            [(send(ref, ref, section=sib), wb.at[h, sib])],
        ]

    def spread_on(h, state):
        a, b = wb.at[h, s_down], wb.at[h, s_up]
        arrive(state[0], a)
        end_a = send(wb.at[h, s_down, lo], wb.at[h, s_down, lo], section=s_up)
        to_sib_a = send(a, a, section=sib)
        arrive(state[1], b)
        end_b = send(wb.at[h, s_up, hi], wb.at[h, s_up, hi], section=s_down)
        to_sib_b = send(b, b, section=sib)
        state[2] += [(to_sib_a, wb.at[h, (sib + 6) % 8]), (to_sib_b, wb.at[h, (sib + 2) % 8])]
        state[:2] = [end_a, end_b]

    def spread_last(h, state):
        arrive(state[0], wb.at[h, s_far, lo])
        arrive(state[1], wb.at[h, s_far, hi])
        ref = wb.at[h, s_far]
        state[2] += [(send(ref, ref, section=sib), wb.at[h, (sib + 4) % 8])]

    arrive(z_up, wb.at[g_down, s])
    far_up = send(wb.at[g_down, s, lo], wb.at[g_down, s, lo], group=g_up)
    pieces[0] = spread(g_down)
    arrive(z_down, wb.at[g_up, s])
    far_down = send(wb.at[g_up, s, hi], wb.at[g_up, s, hi], group=g_down)
    pieces[1] = spread(g_up)
    next(features)
    next(features)
    arrive(far_up, wb.at[g_far, s, lo])
    arrive(far_down, wb.at[g_far, s, hi])
    pieces[2] = spread(g_far)
    text_z = send(tsend, trecv, tp=partner)
    spread_on(g_down, pieces[0])
    spread_on(g_up, pieces[1])
    next(features)
    next(features)
    spread_on(g_far, pieces[2])
    next(features)
    spread_last(g_down, pieces[0])
    spread_last(g_up, pieces[1])
    spread_last(g_far, pieces[2])
    for _ in features:
        pass
    for k in range(3):
        for handle, ref in pieces[k][2]:
            arrive(handle, ref)

    acc[...] = jnp.zeros_like(acc)

    @pl.loop(0, 16)
    def _(k):
        acc[...] += dot(xb[k], wb[k // 4, pl.ds(2 * (k % 4), 2)].reshape(512, 512))

    image = (acc[...] + bias[...]).astype(BF16).astype(F32)
    half = jnp.sum(image * image, axis=1, keepdims=True) * 0.5
    isend[:, :, :KV] = dot((image * gain[...]).astype(BF16), kwv[...]).astype(BF16).reshape(16, 16, KV)
    isend[:, :, KV:] = three_parts(half).reshape(16, 16, PAD)
    parts = [
        send(isend.at[(t + d) % 16], irecv.at[d], tp=(t + d) % 16) for d in range(1, 16)
    ]

    arrive(text_z, trecv)

    @pl.loop(0, 8)
    def _(k):
        total = town[k] + trecv[k].astype(F32)
        town[k] = total
        ysend[k, :, :KV] = total[:, :KV].astype(BF16)
        ysend[k, :, KV:] = three_parts(jnp.sum(total[:, KV:], axis=1, keepdims=True))

    image = isend[t].astype(F32)
    for d in range(1, 16):
        arrive(parts[d - 1], irecv.at[d])
        image += irecv[d].astype(F32)
    scale = inverse_rms(jnp.sum(image[:, KV:], axis=1, keepdims=True))
    ikey[...] = (image[:, :KV] * scale).astype(BF16)
    placed = [send(ikey, dest.at[g], section=s_far, group=(g + d) % 4) for d in range(4)]
    windows = [
        send(ysend.at[(y + d) % 8], yrecv.at[d], tp=2 * ((y + d) % 8) + l) for d in range(1, 8)
    ]

    taken = jnp.int32(0)
    starts = [jnp.int32(1 << 20), jnp.int32(1 << 20)]
    picks = []
    for k in range(4):
        mine = grp[s_far * 4 + k] == g
        start = off[s_far * 4 + k]
        slot = jnp.where(mine, taken, 2)
        picks.append(slot)
        starts = [jnp.where(slot == a, start, starts[a]) for a in range(2)]
        taken = taken + jnp.where(mine, 1, 0)
    for k in range(4):
        arrive(placed[k], dest.at[(g + 4 - k) % 4])
    for a in range(2):
        chosen = jnp.zeros((16, KV), F32)
        for k in range(4):
            chosen = jnp.where(picks[k] == a, dest[k].astype(F32), chosen)
        ag[t, a] = chosen.astype(BF16)
    for _ in ring(ag, ag.at[t]):
        pass

    text = town[y]
    for d in range(1, 8):
        arrive(windows[d - 1], yrecv.at[d])
        text += yrecv[d].astype(F32)
    keys = text[:, :KV] * inverse_rms(jnp.sum(text[:, KV:], axis=1, keepdims=True))
    rows = lax.broadcasted_iota(jnp.int32, (64, 256), 0) + 64 * t
    columns = lax.broadcasted_iota(jnp.int32, (64, 256), 1)
    row = lax.broadcasted_iota(jnp.int32, (64, 1), 0) + 64 * t
    for a in range(2):
        hit = jnp.where(rows - starts[a] == columns, 1.0, 0.0).astype(BF16)
        image = dot(hit, ag[:, a].reshape(256, KV))
        inside = (row >= starts[a]) & (row < starts[a] + 256)
        keys = jnp.where(inside, image, keys)
    out[...] = keys.astype(BF16)

    for copy in sent:
        copy.wait_send()


def on_device(vis, wp, bias, txt, gain, kw, grp, off):
    any_space = pl.BlockSpec(memory_space=pl.ANY)
    vmem = pl.BlockSpec(memory_space=pltpu.VMEM)
    smem = pl.BlockSpec(memory_space=pltpu.SMEM)
    return pl.pallas_call(
        kernel,
        out_shape=jax.ShapeDtypeStruct((64, KV), BF16),
        in_specs=[any_space, any_space, vmem, any_space, vmem, any_space, smem, smem],
        out_specs=vmem,
        scratch_shapes=[
            pltpu.VMEM((16, 256, 512), BF16),
            pltpu.VMEM((4, 8, 256, 512), BF16),
            pltpu.VMEM((8, 2, 64, 512), BF16),
            pltpu.VMEM((512, KV), BF16),
            pltpu.VMEM((8, 64, WIDE), BF16),
            pltpu.VMEM((8, 64, WIDE), BF16),
            pltpu.VMEM((8, 64, WIDE), F32),
            pltpu.VMEM((8, 64, WIDE), BF16),
            pltpu.VMEM((8, 64, WIDE), BF16),
            pltpu.VMEM((256, 512), F32),
            pltpu.VMEM((16, 16, WIDE), BF16),
            pltpu.VMEM((16, 16, WIDE), BF16),
            pltpu.VMEM((16, KV), BF16),
            pltpu.VMEM((4, 16, KV), BF16),
            pltpu.VMEM((16, 2, 16, KV), BF16),
            pltpu.SemaphoreType.DMA((SEMS,)),
            pltpu.SemaphoreType.DMA((SEMS,)),
            pltpu.SemaphoreType.DMA((4,)),
        ],
        compiler_params=pltpu.CompilerParams(
            collective_id=0, has_side_effects=True, vmem_limit_bytes=48 * 1024 * 1024
        ),
    )(
        vis,
        wp.reshape(8, 256, 512),
        bias.astype(F32).reshape(1, 512),
        txt.reshape(8, 2, 64, 512),
        gain.reshape(1, 512),
        kw,
        grp,
        off,
    )


def solution(mesh):
    in_specs = (
        P(("section", "group"), "tp"),
        P("group", "tp"),
        P("tp"),
        P(("section", "group"), "tp"),
        P("tp"),
        P("tp", None),
        P(),
        P(),
    )
    out_specs = P(("section", "group", "tp"), None)
    return jax.shard_map(
        on_device, mesh=mesh, in_specs=in_specs, out_specs=out_specs, check_vma=False
    )
```

time: 490 us -> 142 us (0.29)
  the two profiles are of different devices: /device:TPU:22 before, /device:TPU:2 now
where the time goes in v1:
time: 142 us
  Pallas kernels  134 us (94%)
  local copies, waits for them, and re-layouts  7.64 us (5%)
    pallas_call x1, Pallas kernels, on_device(): pl.pallas_call(kernel, out_shape=jax.ShapeDtypeStruct((64, KV), BF16), in...  134 us
    unnamed x15, local copies, waits for them, and re-layouts  7.64 us

profile of v1, /device:TPU:2, one launch (start us, length us, event | category | flops | bytes accessed | tf_op | source)
XLA Modules:
  0.0 142.1 jit_solution(1103965828952001375)
XLA Ops:
  0.0 0.7 reshape.19
  0.7 0.0 copy-start
  0.7 1.6 %copy-done = bf16[2048,512]{1,0:T(8,128)(2,1)S(1)} copy-done((bf16[2048,512]{1,0:T(8,128)(2,1)S(1)}, bf16[2048,512]{1,0:T(8,128)(2,1)}, u32[]{:S(2)}) %copy-start) | copy-done | bytes 2097176
  2.3 0.0 copy-start.1
  2.3 1.2 copy-done.1
  3.5 0.0 copy-start.2
  3.5 1.2 copy-done.2
  4.7 0.0 copy-start.3
  4.7 0.9 copy-done.3
  5.7 0.0 copy-start.4
  5.7 0.7 copy-done.4
  6.4 0.0 copy-start.5
  6.4 0.7 copy-done.5
  7.0 0.0 copy-start.6
  7.0 0.7 copy-done.6
  7.7 133.8 %shard_map.82 = bf16[64,1024]{1,0:T(8,128)(2,1)S(1)} custom-call(bf16[256,512]{1,0:T(8,128)(2,1)S(1)} %copy-done.3, bf16[8,256,512]{2,1,0:T(8,128)(2,1)S(1)} %bitcast.4, f32[1,512]{1,0:T(1,128)S(1)} %bitcast.6, bf16[8,2,64,512]{3,2,1,0:T(8,128)(2,1)S(1)} %bitcast.5, f32[1,512]{1,0:T(1,128)S(1)} %bitcast.7, bf16[512,1024]{1,0:T(8,128)(2,1)S(1)} %copy-done.2, ...), custom_call_target="tpu_custom_call" | custom-call | tf_op jit(solution)/shard_map/pallas_call | solution.py:282
  141.5 0.7 copy.10
Async XLA Ops:
  0.7 1.6 %copy-start = (bf16[2048,512]{1,0:T(8,128)(2,1)S(1)}, bf16[2048,512]{1,0:T(8,128)(2,1)}, u32[]{:S(2)}) copy-start(bf16[2048,512]{1,0:T(8,128)(2,1)} %param.9) | copy-start | bytes 6291460
  2.3 1.2 copy-start.1
  3.5 1.2 copy-start.2
  4.7 0.9 copy-start.3
  5.7 0.7 copy-start.4
  6.4 0.7 copy-start.5
  7.0 0.7 copy-start.6

commit v2 on v1

v2 whole, which is shorter than its diff:
```python
import jax
import jax.numpy as jnp
from jax import lax
from jax.experimental import pallas as pl
from jax.experimental.pallas import tpu as pltpu
from jax.sharding import PartitionSpec as P

MESH = pl.DeviceIdType.MESH
D = 8192
KV = 1024
PAD = 128
WIDE = KV + PAD
EPS = 1e-05
BIG = 1.9e19
F32 = jnp.float32
BF16 = jnp.bfloat16
SEMS = 128
VMEM_BYTES = 62 * 1024 * 1024


def dot(a, b):
    return jnp.dot(a, b, preferred_element_type=F32)


def three_parts(v):
    lane = lax.broadcasted_iota(jnp.int32, (v.shape[0], PAD), 1)
    hi = v.astype(BF16).astype(F32)
    rest = jnp.where(hi < jnp.inf, v - hi, 0.0)
    mid = rest.astype(BF16).astype(F32)
    low = rest - mid
    parts = jnp.where(lane == 0, hi, jnp.where(lane == 1, mid, jnp.where(lane == 2, low, 0.0)))
    return parts.astype(BF16)


def inverse_rms(half_sum):
    return 1.0 / jnp.sqrt(half_sum * 2.0 / D + EPS)


def kernel(
    vis, wp, bias_in, txt, gain_in, kw, grp_in, off_in, out,
    bias, gain, grp, off, xb, wb, tv, kwv, tsend, trecv, town, csend, crecv, acc, isend, irecv,
    ikey, dest, asend, fin, ssem, rsem, lsem,
):
    s, g, t = lax.axis_index("section"), lax.axis_index("group"), lax.axis_index("tp")
    y, l = t // 2, t % 2
    other = 1 - l
    partner = 2 * y + other
    up, down = 2 * ((y + 1) % 8) + l, 2 * ((y + 7) % 8) + l
    sib = s + 1 - 2 * (s % 2)
    g_up, g_down, g_far = (g + 1) % 4, (g + 3) % 4, (g + 2) % 4
    s_up, s_down, s_far = (s + 2) % 8, (s + 6) % 8, (s + 4) % 8

    local = []
    pairs = (
        (txt, tv), (kw, kwv), (gain_in, gain), (vis, xb.at[t]), (wp, wb.at[pl.ds(8 * g, 8)]),
        (bias_in, bias), (grp_in, grp), (off_in, off),
    )
    for k, (src, dst) in enumerate(pairs):
        copy = pltpu.make_async_copy(src, dst, lsem.at[k])
        copy.start()
        local.append(copy)

    peers = [{"tp": partner}, {"tp": up}, {"tp": down}, {"group": g_up}, {"group": g_down}]
    peers += [{"section": s_up}, {"section": s_down}, {"section": sib}]
    barrier = pltpu.get_barrier_semaphore()
    for peer in peers:
        pl.semaphore_signal(barrier, inc=1, device_id=peer, device_id_type=MESH)
    pl.semaphore_wait(barrier, len(peers))

    sent = []

    def send(src, dst, **peer):
        k = len(sent)
        copy = pltpu.make_async_remote_copy(
            src_ref=src, dst_ref=dst, send_sem=ssem.at[k], recv_sem=rsem.at[k],
            device_id=peer, device_id_type=MESH,
        )
        copy.start()
        sent.append(copy)
        return k, peer

    def pass_on(ref, **peer):
        return send(ref, ref, **peer)

    def arrive(handle, dst):
        k, peer = handle
        pltpu.make_async_remote_copy(
            src_ref=dst, dst_ref=dst, send_sem=ssem.at[k], recv_sem=rsem.at[k],
            device_id=peer, device_id_type=MESH,
        ).wait_recv()

    lo, hi = pl.ds(0, 128), pl.ds(128, 128)

    def block(k, lane):
        return xb.at[2 * ((y + k + 8) % 8) + lane]

    lanes = (l, other)
    right, left = {}, {}

    def ring_start():
        right[0] = send(vis, xb.at[t], tp=up)
        left[0] = send(vis, xb.at[t], tp=down)

    def ring_partner():
        arrive(to_partner, xb.at[partner])
        right[1] = pass_on(xb.at[partner], tp=up)
        left[1] = pass_on(xb.at[partner], tp=down)

    def ring_on(q, step):
        a, b = block(-step, lanes[q]), block(step, lanes[q])
        arrive(right[q], a)
        if step < 3:
            right[q] = pass_on(a, tp=up)
        else:
            right[q] = pass_on(a.at[lo], tp=up)
        arrive(left[q], b)
        if step < 3:
            left[q] = pass_on(b, tp=down)
        else:
            left[q] = pass_on(b.at[hi], tp=down)

    def ring_end(q):
        arrive(right[q], block(4, lanes[q]).at[lo])
        arrive(left[q], block(4, lanes[q]).at[hi])

    groups = {"down": g_down, "up": g_up, "far": g_far}

    def piece(h, section):
        return wb.at[8 * (groups[h] if isinstance(h, str) else h) + section]

    along, to_sib = {}, []

    def spread(h, rows, name):
        ref = piece(h, s).at[rows]
        along[name, h] = (pass_on(ref, section=s_up), pass_on(ref, section=s_down))

    def to_core(h, section, rows=pl.ds(0, 256)):
        handle = pass_on(piece(h, section).at[rows], section=sib)
        to_sib.append((handle, piece(h, (section + sib - s + 8) % 8).at[rows]))

    def spread_on(h):
        arrive(along["lo", h][0], piece(h, s_down).at[lo])
        end_lo = pass_on(piece(h, s_down).at[lo], section=s_up)
        arrive(along["hi", h][1], piece(h, s_up).at[hi])
        end_hi = pass_on(piece(h, s_up).at[hi], section=s_down)
        arrive(along["hi", h][0], piece(h, s_down).at[hi])
        to_core(h, s_down)
        arrive(along["lo", h][1], piece(h, s_up).at[lo])
        to_core(h, s_up)
        along["end", h] = (end_lo, end_hi)

    def spread_end(h):
        arrive(along["end", h][0], piece(h, s_far).at[lo])
        to_core(h, s_far, lo)
        arrive(along["end", h][1], piece(h, s_far).at[hi])
        to_core(h, s_far, hi)

    to_partner = send(vis, xb.at[t], tp=partner)
    ring_start()
    z_up, z_down = {}, {}
    for rows, first in ((lo, 0), (hi, 128)):
        z_up[first] = send(wp.at[s, rows], piece(g, s).at[rows], group=g_up)
        flip = hi if first == 0 else lo
        z_down[128 - first] = send(wp.at[s, flip], piece(g, s).at[flip], group=g_down)

    for k in range(3):
        local[k].wait()

    def text_part(which, j):
        part = tv[pl.ds(4 * j, 4), which].reshape(256, 512).astype(F32)
        part = jnp.minimum(jnp.maximum(part, -BIG), BIG)
        half = jnp.sum(part * part, axis=1, keepdims=True) * 0.5
        part = part * gain[...]
        coarse = part.astype(BF16)
        fine = (part - coarse.astype(F32)).astype(BF16)
        return dot(coarse, kwv[...]) + dot(fine, kwv[...]), half

    @pl.loop(0, 2)
    def _(j):
        keys, half = text_part(other, j)
        tsend[pl.ds(4 * j, 4), :, :KV] = keys.astype(BF16).reshape(4, 64, KV)
        tsend[pl.ds(4 * j, 4), :, KV:] = three_parts(half).reshape(4, 64, PAD)

    ring_on(0, 1)

    @pl.loop(0, 2)
    def _(j):
        keys, half = text_part(l, j)
        lane = lax.broadcasted_iota(jnp.int32, (256, PAD), 1)
        town[pl.ds(4 * j, 4), :, :KV] = keys.reshape(4, 64, KV)
        town[pl.ds(4 * j, 4), :, KV:] = jnp.where(lane == 0, half, 0.0).reshape(4, 64, PAD)

    arrive(z_up[0], piece("down", s).at[lo])
    far_lo = pass_on(piece("down", s).at[lo], group=g_up)
    spread("down", lo, "lo")
    arrive(z_down[128], piece("up", s).at[hi])
    far_hi = pass_on(piece("up", s).at[hi], group=g_down)
    spread("up", hi, "hi")
    ring_partner()
    arrive(z_up[128], piece("down", s).at[hi])
    spread("down", hi, "hi")
    to_core("down", s)
    arrive(z_down[0], piece("up", s).at[lo])
    spread("up", lo, "lo")
    to_core("up", s)
    ring_on(0, 2)
    arrive(far_lo, piece("far", s).at[lo])
    spread("far", lo, "lo")
    arrive(far_hi, piece("far", s).at[hi])
    spread("far", hi, "hi")
    to_core("far", s)
    text_z = send(tsend, trecv, tp=partner)
    ring_on(1, 1)
    spread_on("down")
    spread_on("up")
    ring_on(0, 3)
    ring_on(1, 2)
    spread_on("far")
    spread_end("down")
    spread_end("up")
    ring_on(1, 3)
    spread_end("far")
    for k in range(3, 8):
        local[k].wait()
    for handle, ref in to_sib:
        arrive(handle, ref)

    def project(k):
        w = wb[pl.ds(4 * k, 4)].reshape(1024, 512)
        return dot(xb[2 * k], w[:512]) + dot(xb[2 * k + 1], w[512:])

    acc[...] = jnp.zeros_like(acc) + bias[...].astype(F32)

    @pl.loop(0, 7)
    def _(k):
        acc[...] += project((y + 5 + k) % 8)

    ring_end(0)
    ring_end(1)
    image = (acc[...] + project((y + 4) % 8)).astype(BF16)

    own_start = off[4 * s + g]
    turned = (lax.broadcasted_iota(jnp.int32, (256, 256), 0) - own_start) & 255
    turn = jnp.where(turned == lax.broadcasted_iota(jnp.int32, (256, 256), 1), 1.0, 0.0)
    image = dot(turn.astype(BF16), image)
    half = jnp.sum(image * image, axis=1, keepdims=True) * 0.5
    isend[:, :, KV:] = three_parts(half).reshape(16, 16, PAD)
    isend[:, :, :KV] = dot((image * gain[...]).astype(BF16), kwv[...]).astype(BF16).reshape(16, 16, KV)
    parts = [
        send(isend.at[(t + d) % 16], irecv.at[d], tp=(t + d) % 16) for d in range(1, 16)
    ]

    arrive(text_z, trecv)

    @pl.loop(0, 8)
    def _(k):
        town[k] += trecv[k].astype(F32)

    chain = {}

    def chain_on(step):
        for way, (to, sign) in enumerate(((up, 1), (down, 7))):
            rows = pl.ds(0, 64)
            if step == 1:
                rows = pl.ds(32 * way, 32)
            total = town[(y + sign * (5 - step)) % 8, rows]
            if step == 2:
                first = pl.ds(32 * way, 32)
                arrive(chain[way], crecv.at[way, 0, first])
                came = crecv[way, 0, first].astype(F32)
                empty = jnp.zeros_like(came)
                total += jnp.concatenate([came, empty] if way == 0 else [empty, came], axis=0)
            elif step > 2:
                arrive(chain[way], crecv.at[way, step - 2])
                total += crecv[way, step - 2].astype(F32)
            csend[way, step - 1, rows, :KV] = total[:, :KV].astype(BF16)
            csend[way, step - 1, rows, KV:] = three_parts(
                jnp.sum(total[:, KV:], axis=1, keepdims=True)
            )
            chain[way] = send(
                csend.at[way, step - 1, rows], crecv.at[way, step - 1, rows], tp=to
            )

    chain_on(1)
    image = isend[t].astype(F32)
    for d in range(1, 16):
        arrive(parts[d - 1], irecv.at[d])
        image += irecv[d].astype(F32)
    scale = inverse_rms(jnp.sum(image[:, KV:], axis=1, keepdims=True))
    ikey[...] = (image[:, :KV] * scale).astype(BF16)
    placed = [send(ikey, dest.at[g], section=s_far, group=(g + d) % 4) for d in range(4)]
    chain_on(2)

    starts = [
        jnp.where(grp[s_far * 4 + k] == g, off[s_far * 4 + k], 1 << 20) for k in range(4)
    ]

    def inside(row, k):
        return (row >= starts[k]) & (row < starts[k] + 256)

    for k in range(4):
        arrive(placed[k], dest.at[(g + 4 - k) % 4])
    base = SEMS - 4
    slot = t % 4
    last = []
    for m in range(4):
        row = lax.broadcasted_iota(jnp.int32, (16, 1), 0) + 256 * m + 16 * t
        chosen = jnp.zeros((16, KV), F32)
        for k in range(4):
            chosen = jnp.where(inside(row, k), dest[k].astype(F32), chosen)
        asend[m] = chosen.astype(BF16)
        target = t // 4 + 4 * m
        copy = pltpu.make_async_remote_copy(
            src_ref=asend.at[m], dst_ref=fin.at[slot], send_sem=ssem.at[base + m],
            recv_sem=rsem.at[base + slot], device_id={"tp": target}, device_id_type=MESH,
        )
        last.append((copy, target))

        @pl.when(target != t)
        def _():
            copy.start()

        @pl.when(target == t)
        def _():
            fin[slot] = asend[m]

    chain_on(3)
    chain_on(4)
    text = town[y]
    for way in range(2):
        arrive(chain[way], crecv.at[way, 3])
        text += crecv[way, 3].astype(F32)
    keys = text[:, :KV] * inverse_rms(jnp.sum(text[:, KV:], axis=1, keepdims=True))
    for j in range(4):
        source = 4 * (t % 4) + j

        @pl.when(source != t)
        def _():
            pltpu.make_async_remote_copy(
                src_ref=fin.at[j], dst_ref=fin.at[j], send_sem=ssem.at[base + j],
                recv_sem=rsem.at[base + j], device_id={"tp": source}, device_id_type=MESH,
            ).wait_recv()

    row = lax.broadcasted_iota(jnp.int32, (64, 1), 0) + 64 * t
    hit = inside(row, 0) | inside(row, 1) | inside(row, 2) | inside(row, 3)
    out[...] = jnp.where(hit, fin[...].reshape(64, KV).astype(F32), keys).astype(BF16)

    for copy in sent:
        copy.wait_send()
    for copy, target in last:

        @pl.when(target != t)
        def _():
            copy.wait_send()


def on_device(vis, wp, bias, txt, gain, kw, grp, off):
    return pl.pallas_call(
        kernel,
        out_shape=jax.ShapeDtypeStruct((64, KV), BF16),
        in_specs=[pl.BlockSpec(memory_space=pl.ANY)] * 8,
        out_specs=pl.BlockSpec(memory_space=pltpu.VMEM),
        scratch_shapes=[
            pltpu.VMEM((1, 512), BF16),
            pltpu.VMEM((1, 512), F32),
            pltpu.SMEM((32,), jnp.int32),
            pltpu.SMEM((32,), jnp.int32),
            pltpu.VMEM((16, 256, 512), BF16),
            pltpu.VMEM((32, 256, 512), BF16),
            pltpu.VMEM((8, 2, 64, 512), BF16),
            pltpu.VMEM((512, KV), BF16),
            pltpu.VMEM((8, 64, WIDE), BF16),
            pltpu.VMEM((8, 64, WIDE), BF16),
            pltpu.VMEM((8, 64, WIDE), F32),
            pltpu.VMEM((2, 4, 64, WIDE), BF16),
            pltpu.VMEM((2, 4, 64, WIDE), BF16),
            pltpu.VMEM((256, 512), F32),
            pltpu.VMEM((16, 16, WIDE), BF16),
            pltpu.VMEM((16, 16, WIDE), BF16),
            pltpu.VMEM((16, KV), BF16),
            pltpu.VMEM((4, 16, KV), BF16),
            pltpu.VMEM((4, 16, KV), BF16),
            pltpu.VMEM((4, 16, KV), BF16),
            pltpu.SemaphoreType.DMA((SEMS,)),
            pltpu.SemaphoreType.DMA((SEMS,)),
            pltpu.SemaphoreType.DMA((8,)),
        ],
        compiler_params=pltpu.CompilerParams(
            collective_id=0, has_side_effects=True, vmem_limit_bytes=VMEM_BYTES
        ),
    )(
        vis,
        wp.reshape(8, 256, 512),
        bias.reshape(1, 512),
        txt.reshape(8, 2, 64, 512),
        gain.reshape(1, 512),
        kw,
        grp,
        off,
    )


def solution(mesh):
    in_specs = (
        P(("section", "group"), "tp"),
        P("group", "tp"),
        P("tp"),
        P(("section", "group"), "tp"),
        P("tp"),
        P("tp", None),
        P(),
        P(),
    )
    out_specs = P(("section", "group", "tp"), None)
    return jax.shard_map(
        on_device, mesh=mesh, in_specs=in_specs, out_specs=out_specs, check_vma=False
    )
```

time: 142 us -> 106 us (0.75)
  the two profiles are of different devices: /device:TPU:2 before, /device:TPU:64 now
where the time goes in v2:
time: 106 us
  Pallas kernels  103 us (97%)
  local copies, waits for them, and re-layouts  2.83 us (3%)
    pallas_call x1, Pallas kernels, on_device(): pl.pallas_call(kernel, out_shape=jax.ShapeDtypeStruct((64, KV), BF16), in...  103 us

profile of v2, /device:TPU:64, one launch (start us, length us, event | category | flops | bytes accessed | tf_op | source)
XLA Modules:
  0.0 106.3 jit_solution(16804156902164176703)
XLA Ops:
  0.0 1.3 %reshape.13.bias_in = bf16[1,512]{1,0:T(2,128)(2,1)} reshape(bf16[512]{0:T(512)(128)(2,1)} %param.10) | data formatting | bytes 2048 | tf_op jit(solution)/shard_map/reshape | solution.py:394
  1.3 103.5 %shard_map.82 = bf16[64,1024]{1,0:T(8,128)(2,1)} custom-call(bf16[256,512]{1,0:T(8,128)(2,1)} %vis.1, bf16[8,256,512]{2,1,0:T(8,128)(2,1)} %bitcast.3, bf16[1,512]{1,0:T(2,128)(2,1)} %reshape.13.bias_in, bf16[8,2,64,512]{3,2,1,0:T(8,128)(2,1)} %bitcast.4, f32[1,512]{1,0:T(1,128)} %bitcast.5, bf16[512,1024]{1,0:T(8,128)(2,1)} %kw.1, s32[32]{0:T(128)} %grp_in.1, ...), custom_call_target="tpu_custom_call" | custom-call | tf_op jit(solution)/shard_map/pallas_call | solution.py:358
  104.8 1.6 %copy.10 = bf16[64,1024]{1,0:T(8,128)(2,1)} copy(bf16[64,1024]{1,0:T(8,128)(2,1)} %shard_map.82) | data formatting | bytes 262144

commit v3 on v2

--- a/solution.py
+++ b/solution.py
@@ -95,33 +95,31 @@
         return xb.at[2 * ((y + k + 8) % 8) + lane]
 
     lanes = (l, other)
+    halves = (lo, hi)
     right, left = {}, {}
 
-    def ring_start():
-        right[0] = send(vis, xb.at[t], tp=up)
-        left[0] = send(vis, xb.at[t], tp=down)
-
-    def ring_partner():
-        arrive(to_partner, xb.at[partner])
-        right[1] = pass_on(xb.at[partner], tp=up)
-        left[1] = pass_on(xb.at[partner], tp=down)
-
-    def ring_on(q, step):
-        a, b = block(-step, lanes[q]), block(step, lanes[q])
-        arrive(right[q], a)
-        if step < 3:
-            right[q] = pass_on(a, tp=up)
+    def ring_start(q, half):
+        ref = xb.at[t, halves[half]]
+        if q == 0:
+            src = vis.at[halves[half]]
         else:
-            right[q] = pass_on(a.at[lo], tp=up)
-        arrive(left[q], b)
-        if step < 3:
-            left[q] = pass_on(b, tp=down)
-        else:
-            left[q] = pass_on(b.at[hi], tp=down)
+            arrive(to_partner[half], xb.at[partner, halves[half]])
+            src = ref = xb.at[partner, halves[half]]
+        right[q, half] = send(src, ref, tp=up)
+        left[q, half] = send(src, ref, tp=down)
+
+    def ring_on(q, half, step):
+        a, b = block(-step, lanes[q]).at[halves[half]], block(step, lanes[q]).at[halves[half]]
+        arrive(right[q, half], a)
+        if step < 3 or half == 0:
+            right[q, half] = pass_on(a, tp=up)
+        arrive(left[q, half], b)
+        if step < 3 or half == 1:
+            left[q, half] = pass_on(b, tp=down)
 
     def ring_end(q):
-        arrive(right[q], block(4, lanes[q]).at[lo])
-        arrive(left[q], block(4, lanes[q]).at[hi])
+        arrive(right[q, 0], block(4, lanes[q]).at[lo])
+        arrive(left[q, 1], block(4, lanes[q]).at[hi])
 
     groups = {"down": g_down, "up": g_up, "far": g_far}
 
@@ -155,8 +153,9 @@
         arrive(along["end", h][1], piece(h, s_far).at[hi])
         to_core(h, s_far, hi)
 
-    to_partner = send(vis, xb.at[t], tp=partner)
-    ring_start()
+    to_partner = [send(vis.at[half], xb.at[t, half], tp=partner) for half in halves]
+    ring_start(0, 0)
+    ring_start(0, 1)
     z_up, z_down = {}, {}
     for rows, first in ((lo, 0), (hi, 128)):
         z_up[first] = send(wp.at[s, rows], piece(g, s).at[rows], group=g_up)
@@ -175,87 +174,67 @@
         fine = (part - coarse.astype(F32)).astype(BF16)
         return dot(coarse, kwv[...]) + dot(fine, kwv[...]), half
 
-    @pl.loop(0, 2)
-    def _(j):
+    def text_for_partner(j):
         keys, half = text_part(other, j)
         tsend[pl.ds(4 * j, 4), :, :KV] = keys.astype(BF16).reshape(4, 64, KV)
         tsend[pl.ds(4 * j, 4), :, KV:] = three_parts(half).reshape(4, 64, PAD)
 
-    ring_on(0, 1)
-
-    @pl.loop(0, 2)
-    def _(j):
+    def text_here(j):
         keys, half = text_part(l, j)
         lane = lax.broadcasted_iota(jnp.int32, (256, PAD), 1)
         town[pl.ds(4 * j, 4), :, :KV] = keys.reshape(4, 64, KV)
         town[pl.ds(4 * j, 4), :, KV:] = jnp.where(lane == 0, half, 0.0).reshape(4, 64, PAD)
 
+    text_for_partner(0)
+    ring_on(0, 0, 1)
+    text_for_partner(1)
+    ring_on(0, 1, 1)
+    ring_start(1, 0)
     arrive(z_up[0], piece("down", s).at[lo])
     far_lo = pass_on(piece("down", s).at[lo], group=g_up)
     spread("down", lo, "lo")
     arrive(z_down[128], piece("up", s).at[hi])
     far_hi = pass_on(piece("up", s).at[hi], group=g_down)
     spread("up", hi, "hi")
-    ring_partner()
+    ring_start(1, 1)
+    ring_on(0, 0, 2)
+    text_here(0)
     arrive(z_up[128], piece("down", s).at[hi])
     spread("down", hi, "hi")
     to_core("down", s)
     arrive(z_down[0], piece("up", s).at[lo])
     spread("up", lo, "lo")
     to_core("up", s)
-    ring_on(0, 2)
+    ring_on(1, 0, 1)
+    text_here(1)
+    ring_on(1, 1, 1)
+    ring_on(0, 1, 2)
     arrive(far_lo, piece("far", s).at[lo])
     spread("far", lo, "lo")
     arrive(far_hi, piece("far", s).at[hi])
     spread("far", hi, "hi")
     to_core("far", s)
-    text_z = send(tsend, trecv, tp=partner)
-    ring_on(1, 1)
+    text_z = {}
+    for k in (4, 5, 3, 6, 2, 7, 1, 0):
+        window = (y + k) % 8
+        text_z[k] = send(tsend.at[window], trecv.at[window], tp=partner)
     spread_on("down")
+    ring_on(1, 0, 2)
     spread_on("up")
-    ring_on(0, 3)
-    ring_on(1, 2)
+    ring_on(1, 1, 2)
+    ring_on(0, 0, 3)
+    ring_on(0, 1, 3)
     spread_on("far")
+    ring_on(1, 0, 3)
     spread_end("down")
     spread_end("up")
-    ring_on(1, 3)
+    ring_on(1, 1, 3)
     spread_end("far")
     for k in range(3, 8):
         local[k].wait()
     for handle, ref in to_sib:
         arrive(handle, ref)
 
-    def project(k):
-        w = wb[pl.ds(4 * k, 4)].reshape(1024, 512)
-        return dot(xb[2 * k], w[:512]) + dot(xb[2 * k + 1], w[512:])
-
-    acc[...] = jnp.zeros_like(acc) + bias[...].astype(F32)
-
-    @pl.loop(0, 7)
-    def _(k):
-        acc[...] += project((y + 5 + k) % 8)
-
-    ring_end(0)
-    ring_end(1)
-    image = (acc[...] + project((y + 4) % 8)).astype(BF16)
-
-    own_start = off[4 * s + g]
-    turned = (lax.broadcasted_iota(jnp.int32, (256, 256), 0) - own_start) & 255
-    turn = jnp.where(turned == lax.broadcasted_iota(jnp.int32, (256, 256), 1), 1.0, 0.0)
-    image = dot(turn.astype(BF16), image)
-    half = jnp.sum(image * image, axis=1, keepdims=True) * 0.5
-    isend[:, :, KV:] = three_parts(half).reshape(16, 16, PAD)
-    isend[:, :, :KV] = dot((image * gain[...]).astype(BF16), kwv[...]).astype(BF16).reshape(16, 16, KV)
-    parts = [
-        send(isend.at[(t + d) % 16], irecv.at[d], tp=(t + d) % 16) for d in range(1, 16)
-    ]
-
-    arrive(text_z, trecv)
-
-    @pl.loop(0, 8)
-    def _(k):
-        town[k] += trecv[k].astype(F32)
-
     chain = {}
 
     def chain_on(step):
@@ -263,7 +242,11 @@
             rows = pl.ds(0, 64)
             if step == 1:
                 rows = pl.ds(32 * way, 32)
-            total = town[(y + sign * (5 - step)) % 8, rows]
+            k = sign * (5 - step) % 8
+            window = (y + k) % 8
+            if step > 1 or way == 0:
+                arrive(text_z[k], trecv.at[window])
+            total = town[window, rows] + trecv[window, rows].astype(F32)
             if step == 2:
                 first = pl.ds(32 * way, 32)
                 arrive(chain[way], crecv.at[way, 0, first])
@@ -281,7 +264,33 @@
                 csend.at[way, step - 1, rows], crecv.at[way, step - 1, rows], tp=to
             )
 
+    def project(k):
+        w = wb[pl.ds(4 * k, 4)].reshape(1024, 512)
+        return dot(xb[2 * k], w[:512]) + dot(xb[2 * k + 1], w[512:])
+
+    acc[...] = jnp.zeros_like(acc) + bias[...].astype(F32).reshape(1, 512)
+
+    @pl.loop(0, 7)
+    def _(k):
+        acc[...] += project((y + 5 + k) % 8)
+
     chain_on(1)
+    ring_end(0)
+    ring_end(1)
+    image = (acc[...] + project((y + 4) % 8)).astype(BF16)
+
+    own_start = off[4 * s + g]
+    turned = (lax.broadcasted_iota(jnp.int32, (256, 256), 0) - own_start) & 255
+    turn = jnp.where(turned == lax.broadcasted_iota(jnp.int32, (256, 256), 1), 1.0, 0.0)
+    image = dot(turn.astype(BF16), image)
+    half = jnp.sum(image * image, axis=1, keepdims=True) * 0.5
+    isend[:, :, KV:] = three_parts(half).reshape(16, 16, PAD)
+    isend[:, :, :KV] = dot((image * gain[...]).astype(BF16), kwv[...]).astype(BF16).reshape(16, 16, KV)
+    parts = [
+        send(isend.at[(t + d) % 16], irecv.at[d], tp=(t + d) % 16) for d in range(1, 16)
+    ]
+
+    chain_on(2)
     image = isend[t].astype(F32)
     for d in range(1, 16):
         arrive(parts[d - 1], irecv.at[d])
@@ -289,7 +298,7 @@
     scale = inverse_rms(jnp.sum(image[:, KV:], axis=1, keepdims=True))
     ikey[...] = (image[:, :KV] * scale).astype(BF16)
     placed = [send(ikey, dest.at[g], section=s_far, group=(g + d) % 4) for d in range(4)]
-    chain_on(2)
+    chain_on(3)
 
     starts = [
         jnp.where(grp[s_far * 4 + k] == g, off[s_far * 4 + k], 1 << 20) for k in range(4)
@@ -324,9 +333,9 @@
         def _():
             fin[slot] = asend[m]
 
-    chain_on(3)
     chain_on(4)
-    text = town[y]
+    arrive(text_z[0], trecv.at[y])
+    text = town[y] + trecv[y].astype(F32)
     for way in range(2):
         arrive(chain[way], crecv.at[way, 3])
         text += crecv[way, 3].astype(F32)
@@ -361,7 +370,7 @@
         in_specs=[pl.BlockSpec(memory_space=pl.ANY)] * 8,
         out_specs=pl.BlockSpec(memory_space=pltpu.VMEM),
         scratch_shapes=[
-            pltpu.VMEM((1, 512), BF16),
+            pltpu.VMEM((512,), BF16),
             pltpu.VMEM((1, 512), F32),
             pltpu.SMEM((32,), jnp.int32),
             pltpu.SMEM((32,), jnp.int32),
@@ -391,7 +400,7 @@
     )(
         vis,
         wp.reshape(8, 256, 512),
-        bias.reshape(1, 512),
+        bias,
         txt.reshape(8, 2, 64, 512),
         gain.reshape(1, 512),
         kw,

time: 106 us -> 102 us (0.962)
  the two profiles are of different devices: /device:TPU:64 before, /device:TPU:16 now
where the time goes in v3:
time: 102 us
  Pallas kernels  100 us (98%)
  local copies, waits for them, and re-layouts  1.57 us (2%)
    pallas_call x1, Pallas kernels, on_device(): pl.pallas_call(kernel, out_shape=jax.ShapeDtypeStruct((64, KV), BF16), in...  100 us

profile of v3, /device:TPU:16, one launch (start us, length us, event | category | flops | bytes accessed | tf_op | source)
XLA Modules:
  0.0 102.0 jit_solution(13443660747740152816)
XLA Ops:
  0.0 100.4 %shard_map.82 = bf16[64,1024]{1,0:T(8,128)(2,1)} custom-call(bf16[256,512]{1,0:T(8,128)(2,1)} %vis.1, bf16[8,256,512]{2,1,0:T(8,128)(2,1)} %bitcast.3, bf16[512]{0:T(512)(128)(2,1)} %bias_in.1, bf16[8,2,64,512]{3,2,1,0:T(8,128)(2,1)} %bitcast.4, f32[1,512]{1,0:T(1,128)} %bitcast.5, bf16[512,1024]{1,0:T(8,128)(2,1)} %kw.1, s32[32]{0:T(128)} %grp_in.1, s32[32]{0:T(128)} %off_in.1), custom_call_target="tpu_custom_call" | custom-call | tf_op jit(solution)/shard_map/pallas_call | solution.py:367
  100.4 1.6 %copy.10 = bf16[64,1024]{1,0:T(8,128)(2,1)} copy(bf16[64,1024]{1,0:T(8,128)(2,1)} %shard_map.82) | data formatting | bytes 262144

commit v4 on v3

--- a/solution.py
+++ b/solution.py
@@ -14,7 +14,8 @@
 BIG = 1.9e19
 F32 = jnp.float32
 BF16 = jnp.bfloat16
-SEMS = 128
+NEAR = 512
+SEMS = 144
 VMEM_BYTES = 62 * 1024 * 1024
 
 
@@ -38,7 +39,8 @@
 
 def kernel(
     vis, wp, bias_in, txt, gain_in, kw, grp_in, off_in, out,
-    bias, gain, grp, off, xb, wb, tv, kwv, tsend, trecv, town, csend, crecv, acc, isend, irecv,
+    bias, gain, grp, off, xb, wb, tv, kwv, tsend, trecv, town, csend, crecv, acc, inear, izsend, izrecv,
+    iysend, iyrecv, isend, irecv,
     ikey, dest, asend, fin, ssem, rsem, lsem,
 ):
     s, g, t = lax.axis_index("section"), lax.axis_index("group"), lax.axis_index("tp")
@@ -126,7 +128,7 @@
     def piece(h, section):
         return wb.at[8 * (groups[h] if isinstance(h, str) else h) + section]
 
-    along, to_sib = {}, []
+    along, to_sib = {}, {"down": [], "up": [], "far": []}
 
     def spread(h, rows, name):
         ref = piece(h, s).at[rows]
@@ -134,7 +136,7 @@
 
     def to_core(h, section, rows=pl.ds(0, 256)):
         handle = pass_on(piece(h, section).at[rows], section=sib)
-        to_sib.append((handle, piece(h, (section + sib - s + 8) % 8).at[rows]))
+        to_sib[h].append((handle, piece(h, (section + sib - s + 8) % 8).at[rows]))
 
     def spread_on(h):
         arrive(along["lo", h][0], piece(h, s_down).at[lo])
@@ -153,14 +155,14 @@
         arrive(along["end", h][1], piece(h, s_far).at[hi])
         to_core(h, s_far, hi)
 
-    to_partner = [send(vis.at[half], xb.at[t, half], tp=partner) for half in halves]
     ring_start(0, 0)
     ring_start(0, 1)
-    z_up, z_down = {}, {}
-    for rows, first in ((lo, 0), (hi, 128)):
-        z_up[first] = send(wp.at[s, rows], piece(g, s).at[rows], group=g_up)
-        flip = hi if first == 0 else lo
-        z_down[128 - first] = send(wp.at[s, flip], piece(g, s).at[flip], group=g_down)
+    z_up, z_down, to_partner = {}, {}, []
+    for k, half in enumerate(halves):
+        z_up[k] = send(wp.at[s, half], piece(g, s).at[half], group=g_up)
+        flip = halves[1 - k]
+        z_down[1 - k] = send(wp.at[s, flip], piece(g, s).at[flip], group=g_down)
+        to_partner.append(send(vis.at[half], xb.at[t, half], tp=partner))
 
     for k in range(3):
         local[k].wait()
@@ -189,26 +191,26 @@
     ring_on(0, 0, 1)
     text_for_partner(1)
     ring_on(0, 1, 1)
-    ring_start(1, 0)
     arrive(z_up[0], piece("down", s).at[lo])
     far_lo = pass_on(piece("down", s).at[lo], group=g_up)
     spread("down", lo, "lo")
-    arrive(z_down[128], piece("up", s).at[hi])
+    arrive(z_down[1], piece("up", s).at[hi])
     far_hi = pass_on(piece("up", s).at[hi], group=g_down)
     spread("up", hi, "hi")
-    ring_start(1, 1)
+    ring_start(1, 0)
     ring_on(0, 0, 2)
     text_here(0)
-    arrive(z_up[128], piece("down", s).at[hi])
+    ring_on(0, 1, 2)
+    arrive(z_up[1], piece("down", s).at[hi])
     spread("down", hi, "hi")
     to_core("down", s)
     arrive(z_down[0], piece("up", s).at[lo])
     spread("up", lo, "lo")
     to_core("up", s)
-    ring_on(1, 0, 1)
+    ring_start(1, 1)
+    ring_on(0, 0, 3)
+    ring_on(0, 1, 3)
     text_here(1)
-    ring_on(1, 1, 1)
-    ring_on(0, 1, 2)
     arrive(far_lo, piece("far", s).at[lo])
     spread("far", lo, "lo")
     arrive(far_hi, piece("far", s).at[hi])
@@ -218,22 +220,18 @@
     for k in (4, 5, 3, 6, 2, 7, 1, 0):
         window = (y + k) % 8
         text_z[k] = send(tsend.at[window], trecv.at[window], tp=partner)
+    ring_on(1, 0, 1)
+    ring_on(1, 1, 1)
     spread_on("down")
+    spread_on("up")
     ring_on(1, 0, 2)
-    spread_on("up")
     ring_on(1, 1, 2)
-    ring_on(0, 0, 3)
-    ring_on(0, 1, 3)
     spread_on("far")
     ring_on(1, 0, 3)
+    ring_on(1, 1, 3)
     spread_end("down")
     spread_end("up")
-    ring_on(1, 1, 3)
     spread_end("far")
-    for k in range(3, 8):
-        local[k].wait()
-    for handle, ref in to_sib:
-        arrive(handle, ref)
 
     chain = {}
 
@@ -264,17 +262,30 @@
                 csend.at[way, step - 1, rows], crecv.at[way, step - 1, rows], tp=to
             )
 
+    chain_on(1)
+
+    for k in range(3, 8):
+        local[k].wait()
+
     def project(k):
         w = wb[pl.ds(4 * k, 4)].reshape(1024, 512)
         return dot(xb[2 * k], w[:512]) + dot(xb[2 * k + 1], w[512:])
 
+    def project_group(h):
+        @pl.loop(0, 2)
+        def _(j):
+            @pl.when(2 * h + j != (y + 4) % 8)
+            def _():
+                acc[...] += project(2 * h + j)
+
     acc[...] = jnp.zeros_like(acc) + bias[...].astype(F32).reshape(1, 512)
-
-    @pl.loop(0, 7)
-    def _(k):
-        acc[...] += project((y + 5 + k) % 8)
-
-    chain_on(1)
+    project_group(g)
+    for h in ("down", "up", "far"):
+        for handle, ref in to_sib[h]:
+            arrive(handle, ref)
+        if h == "far":
+            chain_on(2)
+        project_group(groups[h])
     ring_end(0)
     ring_end(1)
     image = (acc[...] + project((y + 4) % 8)).astype(BF16)
@@ -284,17 +295,29 @@
     turn = jnp.where(turned == lax.broadcasted_iota(jnp.int32, (256, 256), 1), 1.0, 0.0)
     image = dot(turn.astype(BF16), image)
     half = jnp.sum(image * image, axis=1, keepdims=True) * 0.5
-    isend[:, :, KV:] = three_parts(half).reshape(16, 16, PAD)
-    isend[:, :, :KV] = dot((image * gain[...]).astype(BF16), kwv[...]).astype(BF16).reshape(16, 16, KV)
+    keys = dot((image * gain[...]).astype(BF16), kwv[...]).astype(BF16)
+    inear[...] = keys[:, :NEAR].reshape(8, 2, 16, NEAR)
+    izsend[...] = inear[:, other]
+    near = send(izsend, izrecv, tp=partner)
+    isend[:, :, : KV - NEAR] = keys[:, NEAR:].reshape(16, 16, KV - NEAR)
+    isend[:, :, KV - NEAR :] = three_parts(half).reshape(16, 16, PAD)
     parts = [
         send(isend.at[(t + d) % 16], irecv.at[d], tp=(t + d) % 16) for d in range(1, 16)
     ]
-
-    chain_on(2)
-    image = isend[t].astype(F32)
+    arrive(near, izrecv)
+    iysend[...] = (inear[:, l].astype(F32) + izrecv[...].astype(F32)).astype(BF16)
+    near = [
+        send(iysend.at[(y + d) % 8], iyrecv.at[d], tp=2 * ((y + d) % 8) + l) for d in range(1, 8)
+    ]
+    first = inear[y, l].astype(F32) + izrecv[y].astype(F32)
+    rest = isend[t].astype(F32)
     for d in range(1, 16):
         arrive(parts[d - 1], irecv.at[d])
-        image += irecv[d].astype(F32)
+        rest += irecv[d].astype(F32)
+    for d in range(1, 8):
+        arrive(near[d - 1], iyrecv.at[d])
+        first += iyrecv[d].astype(F32)
+    image = jnp.concatenate([first, rest], axis=1)
     scale = inverse_rms(jnp.sum(image[:, KV:], axis=1, keepdims=True))
     ikey[...] = (image[:, :KV] * scale).astype(BF16)
     placed = [send(ikey, dest.at[g], section=s_far, group=(g + d) % 4) for d in range(4)]
@@ -384,8 +407,13 @@
             pltpu.VMEM((2, 4, 64, WIDE), BF16),
             pltpu.VMEM((2, 4, 64, WIDE), BF16),
             pltpu.VMEM((256, 512), F32),
-            pltpu.VMEM((16, 16, WIDE), BF16),
-            pltpu.VMEM((16, 16, WIDE), BF16),
+            pltpu.VMEM((8, 2, 16, NEAR), BF16),
+            pltpu.VMEM((8, 16, NEAR), BF16),
+            pltpu.VMEM((8, 16, NEAR), BF16),
+            pltpu.VMEM((8, 16, NEAR), BF16),
+            pltpu.VMEM((8, 16, NEAR), BF16),
+            pltpu.VMEM((16, 16, WIDE - NEAR), BF16),
+            pltpu.VMEM((16, 16, WIDE - NEAR), BF16),
             pltpu.VMEM((16, KV), BF16),
             pltpu.VMEM((4, 16, KV), BF16),
             pltpu.VMEM((4, 16, KV), BF16),

time: 102 us -> 96.1 us (0.942)
  the two profiles are of different devices: /device:TPU:16 before, /device:TPU:8 now
where the time goes in v4:
time: 96.1 us; the launch traced here: 96 us
  Pallas kernels  94.4 us (98%)
  local copies, waits for them, and re-layouts  1.57 us (2%)
    pallas_call x1, Pallas kernels, on_device(): pl.pallas_call(kernel, out_shape=jax.ShapeDtypeStruct((64, KV), BF16), in...  94.4 us

profile of v4, /device:TPU:8, one launch (start us, length us, event | category | flops | bytes accessed | tf_op | source)
XLA Modules:
  0.0 96.0 jit_solution(8267901707307695107)
XLA Ops:
  0.0 94.4 %shard_map.82 = bf16[64,1024]{1,0:T(8,128)(2,1)} custom-call(bf16[256,512]{1,0:T(8,128)(2,1)} %vis.1, bf16[8,256,512]{2,1,0:T(8,128)(2,1)} %bitcast.3, bf16[512]{0:T(512)(128)(2,1)} %bias_in.1, bf16[8,2,64,512]{3,2,1,0:T(8,128)(2,1)} %bitcast.4, f32[1,512]{1,0:T(1,128)} %bitcast.5, bf16[512,1024]{1,0:T(8,128)(2,1)} %kw.1, s32[32]{0:T(128)} %grp_in.1, s32[32]{0:T(128)} %off_in.1), custom_call_target="tpu_custom_call" | custom-call | tf_op jit(solution)/shard_map/pallas_call | solution.py:390
  94.4 1.6 %copy.10 = bf16[64,1024]{1,0:T(8,128)(2,1)} copy(bf16[64,1024]{1,0:T(8,128)(2,1)} %shard_map.82) | data formatting | bytes 262144

commit v5 on v4

--- a/solution.py
+++ b/solution.py
@@ -39,7 +39,7 @@
 
 def kernel(
     vis, wp, bias_in, txt, gain_in, kw, grp_in, off_in, out,
-    bias, gain, grp, off, xb, wb, tv, kwv, tsend, trecv, town, csend, crecv, acc, inear, izsend, izrecv,
+    bias, gain, grp, off, xb, wb, tv, kwv, ssend, srecv, tsend, trecv, town, csend, crecv, acc, inear, izsend, izrecv,
     iysend, iyrecv, isend, irecv,
     ikey, dest, asend, fin, ssem, rsem, lsem,
 ):
@@ -157,12 +157,18 @@
 
     ring_start(0, 0)
     ring_start(0, 1)
-    z_up, z_down, to_partner = {}, {}, []
-    for k, half in enumerate(halves):
+    z_up, z_down = {}, {}
+
+    def weights_out(k):
+        half, flip = halves[k], halves[1 - k]
         z_up[k] = send(wp.at[s, half], piece(g, s).at[half], group=g_up)
-        flip = halves[1 - k]
         z_down[1 - k] = send(wp.at[s, flip], piece(g, s).at[flip], group=g_down)
-        to_partner.append(send(vis.at[half], xb.at[t, half], tp=partner))
+
+    def features_out(k):
+        return send(vis.at[halves[k]], xb.at[t, halves[k]], tp=partner)
+
+    to_partner = [features_out(0)]
+    weights_out(0)
 
     for k in range(3):
         local[k].wait()
@@ -178,8 +184,12 @@
 
     def text_for_partner(j):
         keys, half = text_part(other, j)
-        tsend[pl.ds(4 * j, 4), :, :KV] = keys.astype(BF16).reshape(4, 64, KV)
-        tsend[pl.ds(4 * j, 4), :, KV:] = three_parts(half).reshape(4, 64, PAD)
+        tsend[pl.ds(4 * j, 4)] = keys.astype(BF16).reshape(4, 64, KV)
+        lane = lax.broadcasted_iota(jnp.int32, (64, PAD), 1)
+        squares = jnp.zeros((64, PAD), F32) if j == 0 else ssend[...]
+        for i in range(4):
+            squares = jnp.where(lane == 4 * j + i, half[64 * i : 64 * i + 64], squares)
+        ssend[...] = squares
 
     def text_here(j):
         keys, half = text_part(l, j)
@@ -188,7 +198,12 @@
         town[pl.ds(4 * j, 4), :, KV:] = jnp.where(lane == 0, half, 0.0).reshape(4, 64, PAD)
 
     text_for_partner(0)
+    left_device = (z_up[0][0], z_down[1][0])
+    for k in left_device:
+        sent[k].wait_send()
+    to_partner.append(features_out(1))
     ring_on(0, 0, 1)
+    weights_out(1)
     text_for_partner(1)
     ring_on(0, 1, 1)
     arrive(z_up[0], piece("down", s).at[lo])
@@ -217,6 +232,7 @@
     spread("far", hi, "hi")
     to_core("far", s)
     text_z = {}
+    squares_z = send(ssend, srecv, tp=partner)
     for k in (4, 5, 3, 6, 2, 7, 1, 0):
         window = (y + k) % 8
         text_z[k] = send(tsend.at[window], trecv.at[window], tp=partner)
@@ -235,7 +251,15 @@
 
     chain = {}
 
+    def with_partner(window, rows):
+        lane = lax.broadcasted_iota(jnp.int32, (rows.size, PAD), 1)
+        theirs = jnp.where(lane == window, srecv[rows], 0.0)
+        keys = town[window, rows, :KV] + trecv[window, rows].astype(F32)
+        return jnp.concatenate([keys, town[window, rows, KV:] + theirs], axis=1)
+
     def chain_on(step):
+        if step == 1:
+            arrive(squares_z, srecv)
         for way, (to, sign) in enumerate(((up, 1), (down, 7))):
             rows = pl.ds(0, 64)
             if step == 1:
@@ -244,7 +268,7 @@
             window = (y + k) % 8
             if step > 1 or way == 0:
                 arrive(text_z[k], trecv.at[window])
-            total = town[window, rows] + trecv[window, rows].astype(F32)
+            total = with_partner(window, rows)
             if step == 2:
                 first = pl.ds(32 * way, 32)
                 arrive(chain[way], crecv.at[way, 0, first])
@@ -291,15 +315,18 @@
     image = (acc[...] + project((y + 4) % 8)).astype(BF16)
 
     own_start = off[4 * s + g]
-    turned = (lax.broadcasted_iota(jnp.int32, (256, 256), 0) - own_start) & 255
+    turned = lax.broadcasted_iota(jnp.int32, (256, 256), 0)
+    turned = ((turned & 48) << 2) + ((turned >> 6) << 4) + (turned & 15)
+    turned = (turned - own_start) & 255
     turn = jnp.where(turned == lax.broadcasted_iota(jnp.int32, (256, 256), 1), 1.0, 0.0)
     image = dot(turn.astype(BF16), image)
-    half = jnp.sum(image * image, axis=1, keepdims=True) * 0.5
-    keys = dot((image * gain[...]).astype(BF16), kwv[...]).astype(BF16)
-    inear[...] = keys[:, :NEAR].reshape(8, 2, 16, NEAR)
+    normed = (image * gain[...]).astype(BF16)
+    inear[...] = dot(normed, kwv[:, :NEAR]).astype(BF16).reshape(8, 2, 16, NEAR)
     izsend[...] = inear[:, other]
     near = send(izsend, izrecv, tp=partner)
-    isend[:, :, : KV - NEAR] = keys[:, NEAR:].reshape(16, 16, KV - NEAR)
+    keys = dot(normed, kwv[:, NEAR:]).astype(BF16)
+    isend[:, :, : KV - NEAR] = keys.reshape(16, 16, KV - NEAR)
+    half = jnp.sum(image * image, axis=1, keepdims=True) * 0.5
     isend[:, :, KV - NEAR :] = three_parts(half).reshape(16, 16, PAD)
     parts = [
         send(isend.at[(t + d) % 16], irecv.at[d], tp=(t + d) % 16) for d in range(1, 16)
@@ -311,6 +338,7 @@
     ]
     first = inear[y, l].astype(F32) + izrecv[y].astype(F32)
     rest = isend[t].astype(F32)
+    chain_on(3)
     for d in range(1, 16):
         arrive(parts[d - 1], irecv.at[d])
         rest += irecv[d].astype(F32)
@@ -321,7 +349,8 @@
     scale = inverse_rms(jnp.sum(image[:, KV:], axis=1, keepdims=True))
     ikey[...] = (image[:, :KV] * scale).astype(BF16)
     placed = [send(ikey, dest.at[g], section=s_far, group=(g + d) % 4) for d in range(4)]
-    chain_on(3)
+
+    chain_on(4)
 
     starts = [
         jnp.where(grp[s_far * 4 + k] == g, off[s_far * 4 + k], 1 << 20) for k in range(4)
@@ -332,57 +361,35 @@
 
     for k in range(4):
         arrive(placed[k], dest.at[(g + 4 - k) % 4])
-    base = SEMS - 4
-    slot = t % 4
+    here = 64 * (t % 4) + 16 * (t // 4)
+
+    def chosen(m):
+        row = lax.broadcasted_iota(jnp.int32, (16, 1), 0) + 256 * m + here
+        rows = jnp.zeros((16, KV), F32)
+        for k in range(4):
+            rows = jnp.where(inside(row, k), dest[k].astype(F32), rows)
+        return rows.astype(BF16)
+
     last = []
-    for m in range(4):
-        row = lax.broadcasted_iota(jnp.int32, (16, 1), 0) + 256 * m + 16 * t
-        chosen = jnp.zeros((16, KV), F32)
-        for k in range(4):
-            chosen = jnp.where(inside(row, k), dest[k].astype(F32), chosen)
-        asend[m] = chosen.astype(BF16)
-        target = t // 4 + 4 * m
-        copy = pltpu.make_async_remote_copy(
-            src_ref=asend.at[m], dst_ref=fin.at[slot], send_sem=ssem.at[base + m],
-            recv_sem=rsem.at[base + slot], device_id={"tp": target}, device_id_type=MESH,
-        )
-        last.append((copy, target))
-
-        @pl.when(target != t)
-        def _():
-            copy.start()
-
-        @pl.when(target == t)
-        def _():
-            fin[slot] = asend[m]
-
-    chain_on(4)
+    for d in range(1, 4):
+        target = (t + 4 * d) % 16
+        asend[d] = chosen(target // 4)
+        last.append(send(asend.at[d], fin.at[t // 4], tp=target))
+    fin[t // 4] = chosen(t // 4)
     arrive(text_z[0], trecv.at[y])
-    text = town[y] + trecv[y].astype(F32)
+    text = with_partner(y, pl.ds(0, 64))
     for way in range(2):
         arrive(chain[way], crecv.at[way, 3])
         text += crecv[way, 3].astype(F32)
     keys = text[:, :KV] * inverse_rms(jnp.sum(text[:, KV:], axis=1, keepdims=True))
-    for j in range(4):
-        source = 4 * (t % 4) + j
-
-        @pl.when(source != t)
-        def _():
-            pltpu.make_async_remote_copy(
-                src_ref=fin.at[j], dst_ref=fin.at[j], send_sem=ssem.at[base + j],
-                recv_sem=rsem.at[base + j], device_id={"tp": source}, device_id_type=MESH,
-            ).wait_recv()
-
+    for d in range(1, 4):
+        arrive(last[d - 1], fin.at[((t + 16 - 4 * d) % 16) // 4])
     row = lax.broadcasted_iota(jnp.int32, (64, 1), 0) + 64 * t
     hit = inside(row, 0) | inside(row, 1) | inside(row, 2) | inside(row, 3)
     out[...] = jnp.where(hit, fin[...].reshape(64, KV).astype(F32), keys).astype(BF16)
 
-    for copy in sent:
-        copy.wait_send()
-    for copy, target in last:
-
-        @pl.when(target != t)
-        def _():
+    for k, copy in enumerate(sent):
+        if k not in left_device:
             copy.wait_send()
 
 
@@ -401,8 +408,10 @@
             pltpu.VMEM((32, 256, 512), BF16),
             pltpu.VMEM((8, 2, 64, 512), BF16),
             pltpu.VMEM((512, KV), BF16),
-            pltpu.VMEM((8, 64, WIDE), BF16),
-            pltpu.VMEM((8, 64, WIDE), BF16),
+            pltpu.VMEM((64, PAD), F32),
+            pltpu.VMEM((64, PAD), F32),
+            pltpu.VMEM((8, 64, KV), BF16),
+            pltpu.VMEM((8, 64, KV), BF16),
             pltpu.VMEM((8, 64, WIDE), F32),
             pltpu.VMEM((2, 4, 64, WIDE), BF16),
             pltpu.VMEM((2, 4, 64, WIDE), BF16),

time: 96.1 us -> 94.3 us (0.981)
  the two profiles are of different devices: /device:TPU:8 before, /device:TPU:16 now
where the time goes in v5:
time: 94.3 us; the launch traced here: 94.1 us
  Pallas kernels  92.5 us (98%)
  local copies, waits for them, and re-layouts  1.57 us (2%)
    pallas_call x1, Pallas kernels, on_device(): pl.pallas_call(kernel, out_shape=jax.ShapeDtypeStruct((64, KV), BF16), in...  92.5 us

profile of v5, /device:TPU:16, one launch (start us, length us, event | category | flops | bytes accessed | tf_op | source)
XLA Modules:
  0.0 94.1 jit_solution(1604955131061861736)
XLA Ops:
  0.0 92.5 %shard_map.82 = bf16[64,1024]{1,0:T(8,128)(2,1)} custom-call(bf16[256,512]{1,0:T(8,128)(2,1)} %vis.1, bf16[8,256,512]{2,1,0:T(8,128)(2,1)} %bitcast.3, bf16[512]{0:T(512)(128)(2,1)} %bias_in.1, bf16[8,2,64,512]{3,2,1,0:T(8,128)(2,1)} %bitcast.4, f32[1,512]{1,0:T(1,128)} %bitcast.5, bf16[512,1024]{1,0:T(8,128)(2,1)} %kw.1, s32[32]{0:T(128)} %grp_in.1, s32[32]{0:T(128)} %off_in.1), custom_call_target="tpu_custom_call" | custom-call | tf_op jit(solution)/shard_map/pallas_call | solution.py:397
  92.6 1.6 %copy.10 = bf16[64,1024]{1,0:T(8,128)(2,1)} copy(bf16[64,1024]{1,0:T(8,128)(2,1)} %shard_map.82) | data formatting | bytes 262144

commit v6 on v5

--- a/solution.py
+++ b/solution.py
@@ -14,7 +14,7 @@
 BIG = 1.9e19
 F32 = jnp.float32
 BF16 = jnp.bfloat16
-NEAR = 512
+NEAR = 640
 SEMS = 144
 VMEM_BYTES = 62 * 1024 * 1024
 
@@ -236,10 +236,10 @@
     for k in (4, 5, 3, 6, 2, 7, 1, 0):
         window = (y + k) % 8
         text_z[k] = send(tsend.at[window], trecv.at[window], tp=partner)
+    spread_on("down")
     ring_on(1, 0, 1)
+    spread_on("up")
     ring_on(1, 1, 1)
-    spread_on("down")
-    spread_on("up")
     ring_on(1, 0, 2)
     ring_on(1, 1, 2)
     spread_on("far")
@@ -307,7 +307,7 @@
     for h in ("down", "up", "far"):
         for handle, ref in to_sib[h]:
             arrive(handle, ref)
-        if h == "far":
+        if h == "up":
             chain_on(2)
         project_group(groups[h])
     ring_end(0)

time: 94.3 us -> 92.4 us (0.980)
  Pallas kernels: 92.5 us -> 90.6 us
    pallas_call x1, Pallas kernels: 92.5 us -> 90.6 us  [on_device(): pl.pallas_call(kernel, out_shape=jax.ShapeDtypeStruct((64, KV), BF16), in...]
where the time goes in v6:
time: 92.4 us; the launch traced here: 92.2 us
  Pallas kernels  90.6 us (98%)
  local copies, waits for them, and re-layouts  1.57 us (2%)
    pallas_call x1, Pallas kernels, on_device(): pl.pallas_call(kernel, out_shape=jax.ShapeDtypeStruct((64, KV), BF16), in...  90.6 us

profile of v6, /device:TPU:16, one launch (start us, length us, event | category | flops | bytes accessed | tf_op | source)
XLA Modules:
  0.0 92.2 jit_solution(5900670483361174960)
XLA Ops:
  0.0 90.6 %shard_map.82 = bf16[64,1024]{1,0:T(8,128)(2,1)} custom-call(bf16[256,512]{1,0:T(8,128)(2,1)} %vis.1, bf16[8,256,512]{2,1,0:T(8,128)(2,1)} %bitcast.3, bf16[512]{0:T(512)(128)(2,1)} %bias_in.1, bf16[8,2,64,512]{3,2,1,0:T(8,128)(2,1)} %bitcast.4, f32[1,512]{1,0:T(1,128)} %bitcast.5, bf16[512,1024]{1,0:T(8,128)(2,1)} %kw.1, s32[32]{0:T(128)} %grp_in.1, s32[32]{0:T(128)} %off_in.1), custom_call_target="tpu_custom_call" | custom-call | tf_op jit(solution)/shard_map/pallas_call | solution.py:397
  90.6 1.6 %copy.10 = bf16[64,1024]{1,0:T(8,128)(2,1)} copy(bf16[64,1024]{1,0:T(8,128)(2,1)} %shard_map.82) | data formatting | bytes 262144
